TPU v7x, 32 devices: a whole 2x2x4 slice. The times are simulated.
32 devices in a mesh: mem: 8 (over z, x), gx: 2 (over core), gy: 2 (over y).
Axes of the slice: x: 2, y: 2, z: 4, core: 2. Of those that a mesh axis runs over, the one named last changes fastest.
Arguments:
- fields: float32 [32, 3, 256, 256], P('mem', None, 'gx', 'gy'), may hold values from -3 to 3
- noise: float32 [16, 256, 256], P('mem', 'gx', 'gy'), may hold values from -6 to 6
- ancestors: int32 [2, 2, 16], P('gx', 'gy'), may hold values from 0 to 15
- obs_cells: int32 [2, 2, 256], P('gx', 'gy'), may hold values from 0 to 16383
- obs_values: float32 [2, 2, 256], P('gx', 'gy'), may hold values from -3 to 12
Outputs:
- resampled: float32 [32, 3, 256, 256], P('mem', None, 'gx', 'gy')
- log_weights: float32 [2, 2, 32], P('gx', 'gy', 'mem')
All inputs are finite; a program needn't handle non-finite values.
Results may differ from a plain program's by a relative error of at most 0.00012.
Values sent between devices are 32-bit elements; how exact they have to be, the bound alone decides.
A program may use at most 128 MiB of HBM per device.

v0:
```python
import jax
import jax.numpy as jnp
from jax import lax
from jax.sharding import PartitionSpec as P

COURANT = 0.3
DIFFUSE = 0.05
HYPER = 0.005
NOISE_AMP = 0.1
OBS_VAR = 0.25


def padded_2(block, sides, width):
    for axis, dim in sides:
        count = lax.axis_size(axis)
        forward = [(i, i + 1) for i in range(count - 1)]
        forward.append((count - 1, 0))
        backward = [(target, source) for source, target in forward]
        low = lax.ppermute(
            lax.slice_in_dim(block, block.shape[dim] - width, None, axis=dim), axis, forward
        )
        high = lax.ppermute(lax.slice_in_dim(block, 0, width, axis=dim), axis, backward)
        block = jnp.concatenate([low, block, high], axis=dim)
    return block


def inner(a, width):
    return a[..., width : a.shape[-2] - width, width : a.shape[-1] - width]


def xdiff(a):
    return (a[..., 2:, 1:-1] - a[..., :-2, 1:-1]) * 0.5


def ydiff(a):
    return (a[..., 1:-1, 2:] - a[..., 1:-1, :-2]) * 0.5


def laplace(a):
    return (
        a[..., 2:, 1:-1]
        + a[..., :-2, 1:-1]
        + a[..., 1:-1, 2:]
        + a[..., 1:-1, :-2]
        - 4.0 * a[..., 1:-1, 1:-1]
    )


def smooth(a):
    return DIFFUSE * inner(laplace(a), 1) - HYPER * laplace(laplace(a))


def advance(eta, speed_x, speed_y, force, coriolis):
    depth = 1.0 + eta
    cor_one = coriolis[1:-1]
    u_one = inner(speed_x, 1)
    v_one = inner(speed_y, 1)
    tend_h = xdiff(depth * speed_x) + ydiff(depth * speed_y)
    tend_u = u_one * xdiff(speed_x) + v_one * ydiff(speed_x) + xdiff(eta) - cor_one * v_one
    tend_v = u_one * xdiff(speed_y) + v_one * ydiff(speed_y) + ydiff(eta) + cor_one * u_one
    new_eta = inner(eta, 2) - COURANT * inner(tend_h, 1) + smooth(eta) + NOISE_AMP * force
    new_u = inner(speed_x, 2) - COURANT * inner(tend_u, 1) + smooth(speed_x)
    new_v = inner(speed_y, 2) - COURANT * inner(tend_v, 1) + smooth(speed_y)
    return (new_eta, new_u, new_v)


def coriolis_rows(width, count):
    total_y = count * lax.axis_size("gy")
    first = lax.axis_index("gy") * count
    rows_y = (first + jnp.arange(-width, count + width, dtype=jnp.int32)) % total_y
    return 0.1 + 0.2 * ((rows_y.astype(jnp.float32) + 0.5) / total_y - 0.5)


def take_masked(table, wanted):
    inside = (wanted >= 0) & (wanted < table.shape[0])
    rows = jnp.take(table, jnp.clip(wanted, 0, table.shape[0] - 1), axis=0)
    return jnp.where(inside[:, None], rows, jnp.zeros_like(rows))


def shards(fields, noise, ancestors, obs_cells, obs_values):
    members, comps, count_x, count_y = fields.shape
    force = jnp.repeat(noise, 2, axis=0)
    state = fields
    coriolis = coriolis_rows(2, count_y)
    for step in range(2):
        padded = padded_2(state, (("gx", 2), ("gy", 3)), 2)
        eta, speed_x, speed_y = advance(padded[:, 0], padded[:, 1], padded[:, 2], force, coriolis)
        state = jnp.stack([eta, speed_x, speed_y], axis=1)
    heights = state[:, 0].reshape(members, count_x * count_y)
    observed = jnp.take(heights, obs_cells.reshape(-1), axis=1)
    misfit = observed - obs_values.reshape(1, -1)
    logw = -0.5 * jnp.sum(misfit * misfit, axis=1) / OBS_VAR
    peak = lax.pmax(jnp.max(logw), "mem")
    expo = jnp.exp(logw - peak)
    total = lax.psum(jnp.sum(expo), "mem")
    log_weights = (logw - peak - jnp.log(total)).reshape(1, 1, members)
    flat = state.reshape(members, comps * count_x * count_y)
    lineage = ancestors.reshape(-1)
    member_index = lax.axis_index("mem")
    own_pairs = lax.dynamic_slice_in_dim(lineage, member_index * (members // 2), members // 2)
    source = 2 * jnp.repeat(own_pairs, 2) + jnp.tile(jnp.arange(2, dtype=jnp.int32), members // 2)
    picked = take_masked(lax.all_gather(flat, "mem", axis=0, tiled=True), source)
    resampled = picked.reshape(members, comps, count_x, count_y)
    return (resampled, log_weights)


def solution(mesh):
    return jax.shard_map(
        shards,
        mesh=mesh,
        in_specs=(
            P("mem", None, "gx", "gy"),
            P("mem", "gx", "gy"),
            P("gx", "gy", None),
            P("gx", "gy", None),
            P("gx", "gy", None),
        ),
        out_specs=(P("mem", None, "gx", "gy"), P("gx", "gy", "mem")),
        check_vma=False,
    )
```

profile of v0, /device:TPU:0, one launch (start us, length us, event | category | flops | bytes accessed | tf_op | source)
XLA Modules:
  0.0 171.9 jit_solution(12864311148949374058)
XLA Ops:
  7.2 0.8 fusion.92
  8.1 0.5 collective-permute-start
  8.6 0.1 collective-permute-start.1
  8.7 0.9 broadcast_multiply_fusion
  9.6 1.4 copy.38
  11.1 0.3 copy.37
  11.4 0.3 copy.39
  11.8 0.1 pad_maximum_fusion.11
  11.9 3.0 %collective-permute-start.2 = (f32[4,3,132,2]{2,0,3,1:T(4,128)S(1)}, f32[4,3,132,2]{2,0,3,1:T(4,128)S(1)}, u32[]{:S(2)}, u32[]{:S(2)}) collective-permute-start(f32[4,3,132,2]{2,0,3,1:T(4,128)S(1)} %get-tuple-element.4), channel_id=1, source_target_pairs={{0,1},{1,0},{2,3},{3,2},{4,5},{5,4},{6,7},{7,6},{8,9},{9,8},{10,11... | collective-permute-start | bytes 38024 | tf_op jit(solution)/shard_map/ppermute | solution.py:19
  15.0 0.1 copy.40
  15.2 1.5 collective-permute-done.2
  16.7 2.0 %collective-permute-done.3 = f32[4,3,132,2]{2,0,3,1:T(4,128)S(1)} collective-permute-done((f32[4,3,132,2]{2,0,3,1:T(4,128)S(1)}, f32[4,3,132,2]{2,0,3,1:T(4,128)S(1)}, u32[]{:S(2)}, u32[]{:S(2)}) %collective-permute-start.3) | collective-permute-done | bytes 12704 | tf_op jit(solution)/shard_map/ppermute | solution.py:22
  18.7 1.3 pad_maximum_fusion
  20.0 0.3 slice_bitcast_fusion.4
  20.3 0.3 add_multiply_fusion.3
  20.6 1.2 fusion.100
  21.7 2.3 %fusion.1 = (f32[4,130,130]{1,0,2:T(4,128)S(1)}, f32[4,130,130]{1,0,2:T(4,128)S(1)}, f32[4,130,130]{1,0,2:T(4,128)S(1)}, f32[4,130,130]{1,0,2:T(4,128)S(1)}, f32...) fusion(f32[4,132,132]{1,0,2:T(4,128)S(1)} %get-tuple-element.15, ...), kind=kLoop, calls=%fused_computation.16 | loop fusion | flops 676000 | bytes 5678400 | tf_op jit(solution)/shard_map/sub | solution.py:41
  24.0 0.9 fusion.97
  24.9 0.1 broadcast_in_dim.45
  25.0 1.3 fusion.76
  26.3 2.0 %fusion.60 = f32[4,1,128,128]{2,0,3,1:T(4,128)S(1)} fusion(f32[4,130,130]{1,0,2:T(4,128)S(1)} %get-tuple-element.62, f32[4,130,130]{1,0,2:T(4,128)S(1)} %get-tuple-element.48, f32[4,130,130]{1,0,2:T(4,128)S(1)} %get-tuple-element.49, f32[4,130,130]{1,0,2:T(4,128)S(1)} %get-tuple-element.66, f32[4,130,130]{1,0,2:T(4,128)S(1)} %get-tuple-element.65, ...), kind=kLoop, calls=%fused_computation.107 | loop fusion | flops 1507328 | bytes 3932672 | tf_op jit(solution)/shard_map/stack | solution.py:88
  28.3 2.0 %fusion.45 = f32[4,1,128,128]{2,0,3,1:T(4,128)S(1)} fusion(f32[4,130,130]{1,0,2:T(4,128)S(1)} %get-tuple-element.61, f32[4,130,130]{1,0,2:T(4,128)S(1)} %get-tuple-element.46, f32[4,130,130]{1,0,2:T(4,128)S(1)} %get-tuple-element.47, f32[4,130,130]{1,0,2:T(4,128)S(1)} %get-tuple-element.57, f32[4,130,130]{1,0,2:T(4,128)S(1)} %get-tuple-element.58, ...), kind=kLoop, calls=%fused_computation.86 | loop fusion | flops 1507328 | bytes 3932672 | tf_op jit(solution)/shard_map/stack | solution.py:88
  30.2 0.4 pad_maximum_fusion.2
  30.6 0.5 fusion.91
  31.1 0.3 copy.41
  31.4 0.2 copy.42
  31.6 0.5 collective-permute-start.5
  32.2 0.4 collective-permute-done.4
  32.5 0.3 copy.43
  32.9 0.1 collective-permute-done.5
  33.0 0.3 copy.44
  33.4 0.1 pad_maximum_fusion.8
  33.5 0.3 collective-permute-start.6
  33.8 1.8 %collective-permute-start.7 = (f32[4,3,132,2]{2,0,3,1:T(4,128)S(1)}, f32[4,3,132,2]{2,0,3,1:T(4,128)S(1)}, u32[]{:S(2)}, u32[]{:S(2)}) collective-permute-start(f32[4,3,132,2]{2,0,3,1:T(4,128)S(1)} %get-tuple-element.3), channel_id=1, source_target_pairs={{1,0},{0,1},{3,2},{2,3},{5,4},{4,5},{7,6},{6,7},{9,8},{8,9},{11,10... | collective-permute-start | bytes 38024 | tf_op jit(solution)/shard_map/ppermute | solution.py:22
  35.6 1.8 %collective-permute-done.6 = f32[4,3,132,2]{2,0,3,1:T(4,128)S(1)} collective-permute-done((f32[4,3,132,2]{2,0,3,1:T(4,128)S(1)}, f32[4,3,132,2]{2,0,3,1:T(4,128)S(1)}, u32[]{:S(2)}, u32[]{:S(2)}) %collective-permute-start.6) | collective-permute-done | bytes 12704 | tf_op jit(solution)/shard_map/ppermute | solution.py:19
  37.4 0.3 collective-permute-done.7
  37.6 2.3 %pad_maximum_fusion.1 = f32[4,3,132,132]{2,0,3,1:T(4,128)S(1)} fusion(f32[4,3,132,2]{2,0,3,1:T(4,128)S(1)} %collective-permute-done.7, f32[4,3,2,128]{2,0,3,1:T(4,128)S(1)} %copy.44, f32[4,1,128,128]{2,0,3,1:T(4,128)S(1)} %fusion.45, f32[4,1,128,128]{2,0,3,1:T(4,128)S(1)} %fusion.60, f32[4,1,128,128]{2,0,3,1:T(4,128)S(1)} %fusion.76, ...), kind=kLoop, calls=%fused_computation.3 | loop fusion | flops 1254528 | bytes 1672704 | tf_op jit(solution)/shard_map/concatenate | solution.py:23
  39.9 0.3 slice_bitcast_fusion.1
  40.2 0.3 add_multiply_fusion.1
  40.5 1.2 fusion
  41.7 0.4 fusion.93
  42.0 0.6 fusion.94
  42.6 1.2 fusion.95
  43.8 1.2 fusion.96
  45.0 1.3 fusion.36
  46.3 2.0 %fusion.21 = f32[4,1,128,128]{2,0,3,1:T(4,128)S(1)} fusion(f32[4,130,130]{1,0,2:T(4,128)S(1)} %get-tuple-element.34, f32[4,130,130]{1,0,2:T(4,128)S(1)} %get-tuple-element.27, f32[4,130,130]{1,0,2:T(4,128)S(1)} %get-tuple-element.28, f32[4,130,130]{1,0,2:T(4,128)S(1)} %get-tuple-element.30, f32[4,130,130]{1,0,2:T(4,128)S(1)} %get-tuple-element.31, ...), kind=kLoop, calls=%fused_computation.51 | loop fusion | flops 1507328 | bytes 3932672 | tf_op jit(solution)/shard_map/stack | solution.py:88
  48.2 2.0 %fusion.6 = f32[4,1,128,128]{2,0,3,1:T(4,128)S(1)} fusion(f32[4,130,130]{1,0,2:T(4,128)S(1)} %get-tuple-element.40, f32[4,130,130]{1,0,2:T(4,128)S(1)} %get-tuple-element.25, f32[4,130,130]{1,0,2:T(4,128)S(1)} %get-tuple-element.26, f32[4,130,130]{1,0,2:T(4,128)S(1)} %get-tuple-element.36, f32[4,130,130]{1,0,2:T(4,128)S(1)} %get-tuple-element.37, ...), kind=kLoop, calls=%fused_computation.30 | loop fusion | flops 1507328 | bytes 3932672 | tf_op jit(solution)/shard_map/stack | solution.py:88
  50.2 0.2 pad_maximum_fusion.3
  50.4 0.3 copy.45
  50.7 1.2 reshape.175
  52.1 0.1 min.18
  52.4 7.8 %copy.46 = f32[4,128,128]{0,2,1:T(8,128)} copy(f32[4,128,128]{1,0,2:T(4,128)S(1)} %fusion.36) | data formatting | bytes 524288 | tf_op jit(solution)/shard_map/add | solution.py:61
  60.2 4.8 %gather_fusion.1 = f32[256,4]{1,0:T(8,128)S(1)} fusion(f32[4,16384]{0,1:T(8,128)} %bitcast.57, s32[1024]{0:T(1024)S(1)} %pad_clamp_fusion), kind=kCustom, calls=%fused_computation.1 | custom fusion | bytes 9216 | tf_op jit(solution)/shard_map/jit(_take)/gather | solution.py:90
  65.0 0.2 multiply_reduce_fusion
  65.2 0.6 fusion.90
  65.8 23.2 %pmax.7 = f32[]{:T(128)} all-reduce(f32[]{:T(128)} %fusion.90), channel_id=1, replica_groups=mesh['mem'=8,'gx'=2,'gy'=2] {'mem'}, use_global_device_ids=true, to_apply=%region_2.3 | all-reduce | flops 1 | bytes 8 | tf_op jit(solution)/shard_map/pmax | solution.py:93
  89.0 1.2 exponential_reduce_fusion
  90.2 0.1 and.32
  90.3 18.2 %psum.7 = f32[]{:T(128)} all-reduce(f32[]{:T(128)} %exponential_reduce_fusion), channel_id=1, replica_groups=mesh['mem'=8,'gx'=2,'gy'=2] {'mem'}, use_global_device_ids=true, to_apply=%region_4.5 | all-reduce | flops 1 | bytes 8 | tf_op jit(solution)/shard_map/psum | solution.py:95
  109.2 1.1 subtract_bitcast_fusion
  110.3 42.9 %all-gather.3.cloned.1.call-done = f32[8,4,49152]{2,1,0:T(4,128)} async-done(((f32[1,4,49152]{2,1,0:T(4,128)}), f32[8,4,49152]{2,1,0:T(4,128)}) %all-gather.3.cloned.1.call-update) | async-done | bytes 6291472 | tf_op jit(solution)/shard_map/all_gather | solution.py:102
  153.2 6.8 %reshape.176 = f32[32,49152]{1,0:T(8,128)} reshape(f32[8,4,49152]{2,1,0:T(4,128)} %all-gather.3.cloned.1.call-done) | data formatting | bytes 12582912
  159.9 4.1 %gather_fusion = f32[4,49152]{1,0:T(4,128)S(1)} fusion(f32[32,49152]{1,0:T(8,128)} %reshape.176, s32[1024]{0:T(1024)S(1)} %pad_clamp_fusion.1), kind=kCustom, calls=%fused_computation | custom fusion | bytes 1572880 | tf_op jit(solution)/shard_map/jit(_take)/gather | solution.py:76
  164.1 1.0 select_select_fusion
  (27 shorter events, 0.7 us)
Async XLA Ops:
  7.2 146.0 %all-gather.3.cloned.1.call-start = ((), (), s32[]{:S(2)}) async-start(), calls=%async_computation | async-start | bytes 7077888 | tf_op jit(solution)/shard_map/all_gather | solution.py:102
  8.1 3.0 %collective-permute-start = (f32[4,3,2,128]{3,0,2,1:T(4,128)S(1)}, f32[4,3,2,128]{3,0,2,1:T(4,128)S(1)}, u32[]{:S(2)}, u32[]{:S(2)}) collective-permute-start(f32[4,3,2,128]{3,0,2,1:T(4,128)S(1)} %copy.47), channel_id=1, source_target_pairs={{0,2},{2,0},{1,3},{3,1},{4,6},{6,4},{5,7},{7,5},{8,10},{10,8},{9,1... | collective-permute-start | bytes 36872 | tf_op jit(solution)/shard_map/ppermute | solution.py:19
  8.6 2.8 %collective-permute-start.1 = (f32[4,3,2,128]{3,0,2,1:T(4,128)S(1)}, f32[4,3,2,128]{3,0,2,1:T(4,128)S(1)}, u32[]{:S(2)}, u32[]{:S(2)}) collective-permute-start(f32[4,3,2,128]{3,0,2,1:T(4,128)S(1)} %copy.48), channel_id=1, source_target_pairs={{2,0},{0,2},{3,1},{1,3},{6,4},{4,6},{7,5},{5,7},{10,8},{8,10},{11,... | collective-permute-start | bytes 36872 | tf_op jit(solution)/shard_map/ppermute | solution.py:22
  11.9 4.8 %collective-permute-start.2 = (f32[4,3,132,2]{2,0,3,1:T(4,128)S(1)}, f32[4,3,132,2]{2,0,3,1:T(4,128)S(1)}, u32[]{:S(2)}, u32[]{:S(2)}) collective-permute-start(f32[4,3,132,2]{2,0,3,1:T(4,128)S(1)} %get-tuple-element.4), channel_id=1, source_target_pairs={{0,1},{1,0},{2,3},{3,2},{4,5},{5,4},{6,7},{7,6},{8,9},{9,8},{10,11... | collective-permute-start | bytes 38024 | tf_op jit(solution)/shard_map/ppermute | solution.py:19
  14.9 3.8 %collective-permute-start.3 = (f32[4,3,132,2]{2,0,3,1:T(4,128)S(1)}, f32[4,3,132,2]{2,0,3,1:T(4,128)S(1)}, u32[]{:S(2)}, u32[]{:S(2)}) collective-permute-start(f32[4,3,132,2]{2,0,3,1:T(4,128)S(1)} %get-tuple-element.5), channel_id=1, source_target_pairs={{1,0},{0,1},{3,2},{2,3},{5,4},{4,5},{7,6},{6,7},{9,8},{8,9},{11,10... | collective-permute-start | bytes 38024 | tf_op jit(solution)/shard_map/ppermute | solution.py:22
  31.3 1.2 collective-permute-start.4
  31.6 1.4 collective-permute-start.5
  33.5 3.9 %collective-permute-start.6 = (f32[4,3,132,2]{2,0,3,1:T(4,128)S(1)}, f32[4,3,132,2]{2,0,3,1:T(4,128)S(1)}, u32[]{:S(2)}, u32[]{:S(2)}) collective-permute-start(f32[4,3,132,2]{2,0,3,1:T(4,128)S(1)} %get-tuple-element.2), channel_id=1, source_target_pairs={{0,1},{1,0},{2,3},{3,2},{4,5},{5,4},{6,7},{7,6},{8,9},{9,8},{10,11... | collective-permute-start | bytes 38024 | tf_op jit(solution)/shard_map/ppermute | solution.py:19
  33.8 3.8 %collective-permute-start.7 = (f32[4,3,132,2]{2,0,3,1:T(4,128)S(1)}, f32[4,3,132,2]{2,0,3,1:T(4,128)S(1)}, u32[]{:S(2)}, u32[]{:S(2)}) collective-permute-start(f32[4,3,132,2]{2,0,3,1:T(4,128)S(1)} %get-tuple-element.3), channel_id=1, source_target_pairs={{1,0},{0,1},{3,2},{2,3},{5,4},{4,5},{7,6},{6,7},{9,8},{8,9},{11,10... | collective-permute-start | bytes 38024 | tf_op jit(solution)/shard_map/ppermute | solution.py:22
  50.4 1.6 copy-start.2
  50.4 1.9 %copy-start.1 = (s32[1,1,256]{2,1,0:T(1,128)S(1)}, s32[1,1,256]{2,1,0:T(1,128)}, u32[]{:S(2)}) copy-start(s32[1,1,256]{2,1,0:T(1,128)} %param.8) | copy-start | bytes 3076
  52.4 12.6 %copy-start = (f32[1,1,256]{2,1,0:T(1,128)S(1)}, f32[1,1,256]{2,1,0:T(1,128)}, u32[]{:S(2)}) copy-start(f32[1,1,256]{2,1,0:T(1,128)} %param.9) | copy-start | bytes 3076
Sparse Core Ops, SparseCore 0:
  52.1 101.0 all-gather.2
where the time goes:
time: 172 us
  waiting for transfers between devices  49 us (28%)
  blocking collectives  41.4 us (24%)
  local copies, waits for them, and re-layouts  32.6 us (19%)
  other arithmetic  27.5 us (16%)
  between operations  15 us (9%)
  starting transfers between devices  6.41 us (4%)
    all_gather x1, waiting for transfers between devices, shards(): lax.all_gather(flat, 'mem', axis=0, tiled=True)  42.9 us
    pmax x1, blocking collectives, shards(): peak = lax.pmax(jnp.max(logw), 'mem')  23.2 us
    psum x1, blocking collectives, shards(): total = lax.psum(jnp.sum(expo), 'mem')  18.2 us
    another operation x7, other arithmetic, shards(): state = jnp.stack([eta, speed_x, speed_y], axis=1)  9.66 us
    unnamed x12, local copies, waits for them, and re-layouts  9.54 us
    add x1, local copies, waits for them, and re-layouts, advance(): inner(eta, 2) - COURANT * inner(tend_h, 1) + smooth(eta) + NOISE_AMP * force  7.8 us
    gather x1, local copies, waits for them, and re-layouts, shards(): observed = jnp.take(heights, obs_cells.reshape(-1), axis=1)  4.77 us
    gather x1, local copies, waits for them, and re-layouts, take_masked(): rows = jnp.take(table, jnp.clip(wanted, 0, table.shape[0] - 1), axis=0)  4.06 us
  transfers between devices with their start and end apart: 9, of which 7 were waited for; matrix products, arithmetic and copies ran while one was open for 11% of the time, Pallas kernels for 0%

commit v1 on v0

v1 whole, which is shorter than its diff:
```python
import functools

import jax
import jax.numpy as jnp
from jax import lax
from jax.experimental import pallas as pl
from jax.experimental.pallas import tpu as pltpu
from jax.sharding import PartitionSpec as P

COURANT = 0.3
NOISE_AMP = 0.1
MESH = pl.DeviceIdType.MESH
BASE = 16
EDGE = 8
STRIPE = 32
CHUNK = 16


def roll_y(a, shift):
    return pltpu.roll(a, shift % a.shape[-1], 1)


def advance(get, force, coriolis):
    def parts(comp):
        mid, low, high = get(comp, 0), get(comp, -1), get(comp, 1)
        near = low + high
        far = get(comp, -2) + get(comp, 2)
        left, right = roll_y(mid, 1), roll_y(mid, -1)
        cross = 0.09 * mid - 0.01 * near
        smooth = (
            0.7 * mid
            + 0.09 * near
            - 0.005 * far
            + roll_y(cross - 0.005 * right, -1)
            + roll_y(cross - 0.005 * left, 1)
        )
        return mid, low, high, left, right, smooth

    _, eta_lo, eta_hi, eta_le, eta_ri, eta_s = parts(0)
    u, u_lo, u_hi, u_le, u_ri, u_s = parts(1)
    v, v_lo, v_hi, v_le, v_ri, v_s = parts(2)
    flux = (
        (1.0 + eta_hi) * u_hi
        - (1.0 + eta_lo) * u_lo
        + (1.0 + eta_ri) * v_ri
        - (1.0 + eta_le) * v_le
    )
    half = 0.5 * COURANT
    new_eta = eta_s - half * flux + NOISE_AMP * force
    turn = COURANT * coriolis
    new_u = u_s - half * (u * (u_hi - u_lo) + v * (u_ri - u_le) + (eta_hi - eta_lo)) + turn * v
    new_v = v_s - half * (u * (v_hi - v_lo) + v * (v_ri - v_le) + (eta_ri - eta_le)) - turn * u
    return new_eta, new_u, new_v


def kernel(
    cfg,
    fields_ref,
    noise_ref,
    anc_ref,
    cells_ref,
    values_ref,
    out_ref,
    weights_ref,
    old,
    mid,
    force,
    seam_own,
    seam_old,
    seam_mid,
    seam_new,
    pack_out,
    pack_in,
    logw_out,
    logw_all,
    *rest,
):
    n, inner, outer, members, count_x, count_y = cfg
    pairs = members // 2
    parts = 6
    gathered = rest[0:parts]
    offered = rest[parts : 2 * parts]
    taken = rest[2 * parts : 3 * parts]
    (rim_send, rim_recv, w_send, w_recv, z_send, z_recv, x_send, x_recv) = rest[3 * parts :]

    mem, gx, gy = lax.axis_index("mem"), lax.axis_index("gx"), lax.axis_index("gy")
    place, line = lax.rem(mem, inner), lax.div(mem, inner)
    near_x, near_y, diagonal = (mem, 1 - gx, gy), (mem, gx, 1 - gy), (mem, 1 - gx, 1 - gy)

    barrier = pltpu.get_barrier_semaphore()
    for peer in (near_x, near_y, diagonal):
        pl.semaphore_signal(barrier, inc=1, device_id=peer, device_id_type=MESH)
    for d in range(1, n):
        pl.semaphore_signal(
            barrier, inc=1, device_id=(lax.rem(mem + d, n), gx, gy), device_id_type=MESH
        )

    lane = lax.broadcasted_iota(jnp.int32, (1, count_y), 1)
    spot = lane & (STRIPE - 1)
    owner = lane >> 5
    group = spot >> 2
    packed_comp = jnp.where((group & 1) == 1, group >> 1, ((group >> 1) + 1) & 3)

    def seam_of(rows, size, comp):
        total = jnp.zeros((size, count_y), jnp.float32)
        for m in range(members):
            plane = force[m // 2, rows, :] if comp == 3 else old[m, comp, rows, :]
            low = roll_y(plane, 8 + STRIPE * m)
            high = roll_y(plane, 24 + STRIPE * m)
            total = jnp.where(owner == m, jnp.where(spot < 16, low, high), total)
        return total

    def load(i, carry):
        rows = pl.ds(pl.multiple_of(i * CHUNK, CHUNK), CHUNK)
        padded = pl.ds(pl.multiple_of(i * CHUNK + BASE, CHUNK), CHUNK)
        for m in range(members):
            for comp in range(3):
                old[m, comp, padded, :] = fields_ref[m, comp, rows, :]
        for p in range(pairs):
            force[p, padded, :] = noise_ref[p, rows, :]
        packed = jnp.zeros((CHUNK, count_y), jnp.float32)
        for comp in range(4):
            seam = seam_of(padded, CHUNK, comp)
            seam_own[comp, padded, :] = seam
            packed = jnp.where(packed_comp == comp, roll_y(seam, 8 * comp), packed)
        pack_out[rows, :] = packed
        return carry

    lax.fori_loop(0, count_x // CHUNK, load, 0)
    pl.semaphore_wait(barrier, n + 2)

    top = BASE + count_x
    first, last = pl.ds(0, EDGE), pl.ds(count_x - EDGE, EDGE)
    rim_low, rim_high = pl.ds(BASE - EDGE, EDGE), pl.ds(top, EDGE)
    moves = [
        (pack_out, pack_in.at[pl.ds(BASE, count_x), :], near_y),
        (fields_ref.at[:, :, last, :], old.at[:, :, rim_low, :], near_x),
        (fields_ref.at[:, :, first, :], old.at[:, :, rim_high, :], near_x),
        (noise_ref.at[:, last, :], force.at[:, rim_low, :], near_x),
        (noise_ref.at[:, first, :], force.at[:, rim_high, :], near_x),
        (pack_out.at[last, :], pack_in.at[rim_low, :], diagonal),
        (pack_out.at[first, :], pack_in.at[rim_high, :], diagonal),
    ]
    rims = []
    for k, (src, dst, peer) in enumerate(moves):
        rims.append(
            pltpu.make_async_remote_copy(
                src_ref=src,
                dst_ref=dst,
                send_sem=rim_send.at[k],
                recv_sem=rim_recv.at[k],
                device_id=peer,
                device_id_type=MESH,
            )
        )
    for copy in rims:
        copy.start()
    for copy in rims[1:5]:
        copy.wait_recv()

    total_y = 2 * count_y

    def turning(local):
        rows_y = lax.rem(gy * count_y + local + total_y, total_y)
        return 0.1 + 0.2 * ((rows_y.astype(jnp.float32) + 0.5) / total_y - 0.5)

    cor_tile = turning(lane)
    cor_seam = turning(jnp.where(spot < 16, spot - 8, spot - 24 + count_y))

    wide = (count_x + 2 * EDGE) // CHUNK

    def first_step(i, carry):
        m, at = lax.div(i, wide), pl.multiple_of(lax.rem(i, wide) * CHUNK + EDGE, EDGE)
        new = advance(
            lambda comp, d: old[m, comp, pl.ds(at + d, CHUNK), :],
            force[lax.div(m, 2), pl.ds(at, CHUNK), :],
            cor_tile,
        )
        for comp in range(3):
            mid[m, comp, pl.ds(at, CHUNK), :] = new[comp]
        return carry

    lax.fori_loop(0, members * wide, first_step, 0)

    for start in (BASE - EDGE, top):
        rows = pl.ds(start, EDGE)
        for comp in range(4):
            seam_own[comp, rows, :] = seam_of(rows, EDGE, comp)
    for copy in (rims[0], rims[5], rims[6]):
        copy.wait_recv()

    def seam_fill(i, carry):
        rows = pl.ds(pl.multiple_of(i * CHUNK + EDGE, EDGE), CHUNK)
        packed = pack_in[rows, :]
        for comp in range(4):
            seam_old[comp, rows, :] = jnp.where(
                (spot >= 8) & (spot < 24), seam_own[comp, rows, :], roll_y(packed, -8 * comp)
            )
        return carry

    lax.fori_loop(0, wide, seam_fill, 0)

    def seam_step(source, target):
        def body(i, carry):
            at = pl.multiple_of(i * CHUNK + EDGE, EDGE)
            new = advance(
                lambda comp, d: source[comp, pl.ds(at + d, CHUNK), :],
                seam_old[3, pl.ds(at, CHUNK), :],
                cor_seam,
            )
            for comp in range(3):
                target[comp, pl.ds(at, CHUNK), :] = new[comp]
            return carry

        lax.fori_loop(0, wide, body, 0)

    seam_step(seam_old, seam_mid)
    seam_step(seam_mid, seam_new)

    def z_copy(part, origin, right):
        way = 0 if right else 1
        peer = line + 1 if right else line - 1
        block = gathered[part].at[origin]
        return pltpu.make_async_remote_copy(
            src_ref=block,
            dst_ref=block,
            send_sem=z_send.at[way, part, origin],
            recv_sem=z_recv.at[way, part, origin],
            device_id=(peer * inner + place, gx, gy),
            device_id_type=MESH,
        )

    for e in range(2):
        for p in range(pairs):
            m = 2 * p + e

            def second_step(i, carry, m=m, p=p, e=e):
                row = pl.multiple_of(i * CHUNK, CHUNK)
                at = row + BASE
                new = advance(
                    lambda comp, d: mid[m, comp, pl.ds(at + d, CHUNK), :],
                    force[p, pl.ds(at, CHUNK), :],
                    cor_tile,
                )
                for comp in range(3):
                    seam = seam_new[comp, pl.ds(at, CHUNK), :]
                    low, high = roll_y(seam, -(STRIPE * m + 8)), roll_y(seam, -(STRIPE * m + 24))
                    whole = jnp.where(lane < 4, low, jnp.where(lane >= count_y - 4, high, new[comp]))
                    gathered[3 * e + comp][line, p, pl.ds(row, CHUNK), :] = whole
                return carry

            lax.fori_loop(0, count_x // CHUNK, second_step, 0)
        for comp in range(3):
            part = 3 * e + comp

            @pl.when(line < outer - 1)
            def _(part=part):
                z_copy(part, line, True).start()

            @pl.when(line > 0)
            def _(part=part):
                z_copy(part, line, False).start()

    cells = cells_ref[...]
    hot_y = jnp.where(
        lax.broadcasted_iota(jnp.int32, (count_y, cells.shape[1]), 0) == lax.rem(cells, count_y),
        1.0,
        0.0,
    )
    hot_x = lax.broadcasted_iota(jnp.int32, (count_x, cells.shape[1]), 0) == lax.div(cells, count_y)
    tile_lane = lax.broadcasted_iota(jnp.int32, (8, 128), 1)
    own = jnp.zeros((8, 128), jnp.float32)
    for m in range(members):
        picked = jnp.dot(
            gathered[3 * (m % 2)][line, m // 2],
            hot_y,
            precision=lax.Precision.HIGHEST,
            preferred_element_type=jnp.float32,
        )
        seen = jnp.sum(jnp.where(hot_x, picked, 0.0), axis=0, keepdims=True)
        misfit = seen - values_ref[...]
        logw = -2.0 * jnp.sum(misfit * misfit, axis=1, keepdims=True)
        own = jnp.where(tile_lane == m, logw, own)
    logw_out[...] = own
    logw_all[mem] = own

    def w_copy(d):
        return pltpu.make_async_remote_copy(
            src_ref=logw_out,
            dst_ref=logw_all.at[mem],
            send_sem=w_send.at[d],
            recv_sem=w_recv.at[d],
            device_id=(lax.rem(mem + d, n), gx, gy),
            device_id_type=MESH,
        )

    for d in range(1, n):
        w_copy(d).start()

    def x_copy(part, d):
        return pltpu.make_async_remote_copy(
            src_ref=offered[part].at[d],
            dst_ref=taken[part].at[place],
            send_sem=x_send.at[part, d],
            recv_sem=x_recv.at[part, d],
            device_id=(line * inner + lax.rem(place + d, inner), gx, gy),
            device_id_type=MESH,
        )

    def finish(part):
        e, comp = part // 3, part % 3
        for d in range(1, inner):
            x_copy(part, d).wait_recv()
        for s in range(pairs):
            source = lax.rem(lax.div(anc_ref[0, mem * pairs + s], pairs), inner)
            out_ref[2 * s + e, comp] = taken[part][source, s]

    for part in range(parts):
        for t in range(1, outer):

            @pl.when(line - t >= 0)
            def _(part=part, t=t):
                z_copy(part, line - t, True).wait_recv()

                @pl.when(line < outer - 1)
                def _():
                    z_copy(part, line - t, True).start()

            @pl.when(line + t < outer)
            def _(part=part, t=t):
                z_copy(part, line + t, False).wait_recv()

                @pl.when(line > 0)
                def _():
                    z_copy(part, line + t, False).start()

        for d in range(inner):
            goal = line * inner + lax.rem(place + d, inner)
            for s in range(pairs):
                wanted = anc_ref[0, goal * pairs + s]
                origin = lax.div(lax.div(wanted, pairs), inner)
                block = gathered[part][origin, lax.rem(wanted, pairs)]
                if d == 0:
                    taken[part][place, s] = block
                else:
                    offered[part][d, s] = block
            if d > 0:
                x_copy(part, d).start()
        if part > 0:
            finish(part - 1)
    finish(parts - 1)

    for d in range(1, n):
        w_copy(d).wait_recv()
    every = logw_all[...]
    real = lax.broadcasted_iota(jnp.int32, every.shape, 2) < members
    once = lax.broadcasted_iota(jnp.int32, every.shape, 1) == 0
    every_max = jnp.max(jnp.where(real, every, -jnp.inf), axis=0)
    peak = jnp.max(every_max, axis=1, keepdims=True)
    expo = jnp.where(real & once, jnp.exp(jnp.where(real, every - peak[None], 0.0)), 0.0)
    total = jnp.sum(jnp.sum(jnp.sum(expo, axis=0), axis=1, keepdims=True), axis=0, keepdims=True)
    normal = own - peak - jnp.log(total)
    weights_ref[...] = normal[0:1, 0:members]

    for copy in rims:
        copy.wait_send()
    for d in range(1, n):
        w_copy(d).wait_send()
    for part in range(parts):
        for d in range(1, inner):
            x_copy(part, d).wait_send()
        for t in range(outer):

            @pl.when((line - t >= 0) & (line < outer - 1))
            def _(part=part, t=t):
                z_copy(part, line - t, True).wait_send()

            @pl.when((line + t < outer) & (line > 0))
            def _(part=part, t=t):
                z_copy(part, line + t, False).wait_send()


def shards(n, fields, noise, ancestors, obs_cells, obs_values):
    members, comps, count_x, count_y = fields.shape
    inner = 1
    while inner * inner * 4 <= n:
        inner *= 2
    outer = n // inner
    pairs = members // 2
    rows = count_x + 2 * BASE
    f32 = jnp.float32
    vmem = pl.BlockSpec(memory_space=pltpu.VMEM)
    dma = pltpu.SemaphoreType.DMA
    parts = 2 * comps
    plane = (count_x, count_y)
    scratch = [
        pltpu.VMEM((members, 3, rows, count_y), f32),
        pltpu.VMEM((members, 3, rows, count_y), f32),
        pltpu.VMEM((pairs, rows, count_y), f32),
        pltpu.VMEM((4, rows, count_y), f32),
        pltpu.VMEM((4, rows, count_y), f32),
        pltpu.VMEM((3, rows, count_y), f32),
        pltpu.VMEM((3, rows, count_y), f32),
        pltpu.VMEM(plane, f32),
        pltpu.VMEM((rows, count_y), f32),
        pltpu.VMEM((8, 128), f32),
        pltpu.VMEM((n, 8, 128), f32),
    ]
    scratch += [pltpu.VMEM((outer, pairs) + plane, f32)] * parts
    scratch += [pltpu.VMEM((inner, pairs) + plane, f32)] * (2 * parts)
    scratch += [
        dma((7,)),
        dma((7,)),
        dma((n,)),
        dma((n,)),
        dma((2, parts, outer)),
        dma((2, parts, outer)),
        dma((parts, inner)),
        dma((parts, inner)),
    ]
    resampled, weights = pl.pallas_call(
        functools.partial(kernel, (n, inner, outer, members, count_x, count_y)),
        out_shape=(
            jax.ShapeDtypeStruct(fields.shape, f32),
            jax.ShapeDtypeStruct((1, members), f32),
        ),
        in_specs=[vmem, vmem, pl.BlockSpec(memory_space=pltpu.SMEM), vmem, vmem],
        out_specs=(vmem, vmem),
        scratch_shapes=scratch,
        compiler_params=pltpu.CompilerParams(
            collective_id=0, has_side_effects=True, vmem_limit_bytes=48 * 1024 * 1024
        ),
    )(
        fields,
        noise,
        ancestors.reshape(1, -1),
        obs_cells.reshape(1, -1),
        obs_values.reshape(1, -1),
    )
    return resampled, weights.reshape(1, 1, members)


def solution(mesh):
    return jax.shard_map(
        functools.partial(shards, mesh.shape["mem"]),
        mesh=mesh,
        in_specs=(
            P("mem", None, "gx", "gy"),
            P("mem", "gx", "gy"),
            P("gx", "gy", None),
            P("gx", "gy", None),
            P("gx", "gy", None),
        ),
        out_specs=(P("mem", None, "gx", "gy"), P("gx", "gy", "mem")),
        check_vma=False,
    )
```

time: 172 us -> 83.8 us (0.49)
  Pallas kernels: 0 us -> 78.8 us
  waiting for transfers between devices: 49 us -> 0 us
  blocking collectives: 41.4 us -> 0 us
  local copies, waits for them, and re-layouts: 32.6 us -> 4.1 us
  other arithmetic: 27.5 us -> 0 us
  between operations: 15 us -> 0.67 us
  starting transfers between devices: 6.41 us -> 0 us
    pallas_call x0 -> x1, Pallas kernels: none -> 78.8 us  [shards(): pl.pallas_call(functools.partial(kernel, (n, inner, outer, members, count...]
    all_gather x1 -> x0, waiting for transfers between devices: 42.9 us -> none  [shards(): lax.all_gather(flat, 'mem', axis=0, tiled=True)]
    pmax x1 -> x0, blocking collectives: 23.2 us -> none  [shards(): peak = lax.pmax(jnp.max(logw), 'mem')]
    psum x1 -> x0, blocking collectives: 18.2 us -> none  [shards(): total = lax.psum(jnp.sum(expo), 'mem')]
    another operation x7 -> x0, other arithmetic: 9.66 us -> none  [shards(): state = jnp.stack([eta, speed_x, speed_y], axis=1)]
    gather x2 -> x0, local copies, waits for them, and re-layouts: 8.83 us -> none  [the longest x1 4.77 us: shards(): observed = jnp.take(heights, obs_cells.reshape(-1), axis=1)]
    add x1 -> x0, local copies, waits for them, and re-layouts: 7.8 us -> none  [advance(): inner(eta, 2) - COURANT * inner(tend_h, 1) + smooth(eta) + NOISE_AMP * force]
    ppermute x8 -> x0, starting transfers between devices: 6.37 us -> none  [the longest x4 3.9 us: padded_2(): lax.ppermute(lax.slice_in_dim(block, block.shape[dim] - width, None, axis...]
  transfers between devices with their start and end apart: 9 -> 0, of which waited for: 7 -> 0; matrix products, arithmetic and copies ran while one was open for 11% -> 0% of each run, Pallas kernels for 0% -> 0%
where the time goes in v1:
time: 83.8 us; the launch traced here: 83.6 us
  Pallas kernels  78.8 us (94%)
  local copies, waits for them, and re-layouts  4.1 us (5%)
    pallas_call x1, Pallas kernels, shards(): pl.pallas_call(functools.partial(kernel, (n, inner, outer, members, count...  78.8 us
    unnamed x12, local copies, waits for them, and re-layouts  4.1 us

profile of v1, /device:TPU:0, one launch (start us, length us, event | category | flops | bytes accessed | tf_op | source)
XLA Modules:
  0.0 83.6 jit_solution(7822196230680561888)
XLA Ops:
  0.6 0.0 copy-start.3
  0.6 0.0 copy-start.2
  0.7 0.0 copy-start.4
  0.7 0.7 copy-done.3
  1.3 0.0 copy-done.2
  1.3 0.0 copy-done.4
  1.3 0.0 copy-start
  1.3 1.1 %copy-done = f32[4,3,128,128]{3,2,1,0:T(8,128)S(1)} copy-done((f32[4,3,128,128]{3,2,1,0:T(8,128)S(1)}, f32[4,3,128,128]{3,2,1,0:T(8,128)}, u32[]{:S(2)}) %copy-start) | copy-done | bytes 786456
  2.5 0.0 copy-start.1
  2.5 0.9 %copy-done.1 = f32[2,128,128]{2,1,0:T(8,128)S(1)} copy-done((f32[2,128,128]{2,1,0:T(8,128)S(1)}, f32[2,128,128]{2,1,0:T(8,128)}, u32[]{:S(2)}) %copy-start.1) | copy-done | bytes 131096
  3.4 78.8 %shard_map.68 = (f32[4,3,128,128]{3,2,1,0:T(8,128)S(1)}, f32[1,4]{1,0:T(1,128)S(1)}) custom-call(f32[4,3,128,128]{3,2,1,0:T(8,128)S(1)} %copy-done, f32[2,128,128]{2,1,0:T(8,128)S(1)} %copy-done.1, s32[1,16]{1,0:T(1,128)S(1)} %bitcast.6, s32[1,256]{1,0:T(1,128)S(1)} %bitcast.4, f32[1,256]{1,0:T(1,128)S(1)} %bitcast.5), custom_call_target="tpu_custom_call" | custom-call | tf_op jit(solution)/shard_map/pallas_call | solution.py:421
  82.2 0.9 %copy.9 = f32[4,3,128,128]{3,2,1,0:T(8,128)} copy(f32[4,3,128,128]{3,2,1,0:T(8,128)S(1)} %get-tuple-element.8) | data formatting | bytes 1572864
  83.1 0.5 copy.10
Async XLA Ops:
  0.6 0.7 copy-start.3
  0.6 0.7 copy-start.2
  0.7 0.7 copy-start.4
  1.3 1.1 %copy-start = (f32[4,3,128,128]{3,2,1,0:T(8,128)S(1)}, f32[4,3,128,128]{3,2,1,0:T(8,128)}, u32[]{:S(2)}) copy-start(f32[4,3,128,128]{3,2,1,0:T(8,128)} %fields_ref.1) | copy-start | bytes 2359300
  2.5 0.9 %copy-start.1 = (f32[2,128,128]{2,1,0:T(8,128)S(1)}, f32[2,128,128]{2,1,0:T(8,128)}, u32[]{:S(2)}) copy-start(f32[2,128,128]{2,1,0:T(8,128)} %noise_ref.1) | copy-start | bytes 393220

commit v2 on v1

--- a/solution.py
+++ b/solution.py
@@ -81,7 +81,10 @@
     gathered = rest[0:parts]
     offered = rest[parts : 2 * parts]
     taken = rest[2 * parts : 3 * parts]
-    (rim_send, rim_recv, w_send, w_recv, z_send, z_recv, x_send, x_recv) = rest[3 * parts :]
+    end_out = rest[3 * parts : 4 * parts]
+    end_in = rest[4 * parts : 5 * parts]
+    (rim_send, rim_recv, w_send, w_recv, z_send, z_recv) = rest[5 * parts : 5 * parts + 6]
+    (x_send, x_recv, end_send, end_recv) = rest[5 * parts + 6 :]
 
     mem, gx, gy = lax.axis_index("mem"), lax.axis_index("gx"), lax.axis_index("gy")
     place, line = lax.rem(mem, inner), lax.div(mem, inner)
@@ -169,18 +172,22 @@
 
     wide = (count_x + 2 * EDGE) // CHUNK
 
-    def first_step(i, carry):
-        m, at = lax.div(i, wide), pl.multiple_of(lax.rem(i, wide) * CHUNK + EDGE, EDGE)
-        new = advance(
-            lambda comp, d: old[m, comp, pl.ds(at + d, CHUNK), :],
-            force[lax.div(m, 2), pl.ds(at, CHUNK), :],
-            cor_tile,
-        )
-        for comp in range(3):
-            mid[m, comp, pl.ds(at, CHUNK), :] = new[comp]
-        return carry
-
-    lax.fori_loop(0, members * wide, first_step, 0)
+    def first_step(e):
+        def body(i, carry):
+            p, at = lax.div(i, wide), pl.multiple_of(lax.rem(i, wide) * CHUNK + EDGE, EDGE)
+            m = 2 * p + e
+            new = advance(
+                lambda comp, d: old[m, comp, pl.ds(at + d, CHUNK), :],
+                force[p, pl.ds(at, CHUNK), :],
+                cor_tile,
+            )
+            for comp in range(3):
+                mid[m, comp, pl.ds(at, CHUNK), :] = new[comp]
+            return carry
+
+        lax.fori_loop(0, pairs * wide, body, 0, unroll=3)
+
+    first_step(0)
 
     for start in (BASE - EDGE, top):
         rows = pl.ds(start, EDGE)
@@ -212,7 +219,7 @@
                 target[comp, pl.ds(at, CHUNK), :] = new[comp]
             return carry
 
-        lax.fori_loop(0, wide, body, 0)
+        lax.fori_loop(0, wide, body, 0, unroll=3)
 
     seam_step(seam_old, seam_mid)
     seam_step(seam_mid, seam_new)
@@ -230,7 +237,24 @@
             device_id_type=MESH,
         )
 
+    at_end = (line == 0) | (line == outer - 1)
+
+    def start_own(part, when):
+        go_right, go_left = line < outer - 2, line > 1
+        if when is not None:
+            go_right, go_left = go_right & when, go_left & when
+
+        @pl.when(go_right)
+        def _():
+            z_copy(part, line, True).start()
+
+        @pl.when(go_left)
+        def _():
+            z_copy(part, line, False).start()
+
     for e in range(2):
+        if e == 1:
+            first_step(1)
         for p in range(pairs):
             m = 2 * p + e
 
@@ -249,17 +273,9 @@
                     gathered[3 * e + comp][line, p, pl.ds(row, CHUNK), :] = whole
                 return carry
 
-            lax.fori_loop(0, count_x // CHUNK, second_step, 0)
+            lax.fori_loop(0, count_x // CHUNK, second_step, 0, unroll=2)
         for comp in range(3):
-            part = 3 * e + comp
-
-            @pl.when(line < outer - 1)
-            def _(part=part):
-                z_copy(part, line, True).start()
-
-            @pl.when(line > 0)
-            def _(part=part):
-                z_copy(part, line, False).start()
+            start_own(3 * e + comp, None if e == 0 else at_end)
 
     cells = cells_ref[...]
     hot_y = jnp.where(
@@ -315,39 +331,89 @@
             source = lax.rem(lax.div(anc_ref[0, mem * pairs + s], pairs), inner)
             out_ref[2 * s + e, comp] = taken[part][source, s]
 
-    for part in range(parts):
+    def end_copy(part):
+        end = jnp.where(line == 1, 0, outer - 1)
+        return pltpu.make_async_remote_copy(
+            src_ref=end_out[part],
+            dst_ref=end_in[part],
+            send_sem=end_send.at[part],
+            recv_sem=end_recv.at[part],
+            device_id=(end * inner + place, gx, gy),
+            device_id_type=MESH,
+        )
+
+    def pick(part, wanted):
+        origin = lax.div(lax.div(wanted, pairs), inner)
+        return gathered[part][origin, lax.rem(wanted, pairs)]
+
+    def deliver(part):
+        @pl.when((line == 1) | (line == outer - 2))
+        def _():
+            end = jnp.where(line == 1, 0, outer - 1)
+            for k in range(inner * pairs):
+                end_out[part][k] = pick(part, anc_ref[0, end * inner * pairs + k])
+            end_copy(part).start()
+
+        def place_block(d, s, block):
+            if d == 0:
+                taken[part][place, s] = block
+            else:
+                offered[part][d, s] = block
+
+        @pl.when(jnp.logical_not(at_end))
+        def _():
+            for d in range(inner):
+                goal = line * inner + lax.rem(place + d, inner)
+                for s in range(pairs):
+                    place_block(d, s, pick(part, anc_ref[0, goal * pairs + s]))
+
+        @pl.when(at_end)
+        def _():
+            end_copy(part).wait_recv()
+            for d in range(inner):
+                spot_in = lax.rem(place + d, inner)
+                for s in range(pairs):
+                    wanted = anc_ref[0, (line * inner + spot_in) * pairs + s]
+                    origin = lax.div(lax.div(wanted, pairs), inner)
+                    here = gathered[part][line, 0]
+                    for p in range(1, pairs):
+                        here = jnp.where(lax.rem(wanted, pairs) == p, gathered[part][line, p], here)
+                    sent = end_in[part][spot_in * pairs + s]
+                    place_block(d, s, jnp.where(origin == line, here, sent))
+
+        for d in range(1, inner):
+            x_copy(part, d).start()
+
+    middle = jnp.logical_not(at_end)
+    for turn in range(parts + outer - 2):
         for t in range(1, outer):
-
-            @pl.when(line - t >= 0)
+            part = turn - (t - 1)
+            if not 0 <= part < parts:
+                continue
+
+            @pl.when((line - t >= 0) & (line < outer - 1))
             def _(part=part, t=t):
                 z_copy(part, line - t, True).wait_recv()
 
-                @pl.when(line < outer - 1)
+                @pl.when(line < outer - 2)
                 def _():
                     z_copy(part, line - t, True).start()
 
-            @pl.when(line + t < outer)
+            @pl.when((line + t < outer) & (line > 0))
             def _(part=part, t=t):
                 z_copy(part, line + t, False).wait_recv()
 
-                @pl.when(line > 0)
+                @pl.when(line > 1)
                 def _():
                     z_copy(part, line + t, False).start()
 
-        for d in range(inner):
-            goal = line * inner + lax.rem(place + d, inner)
-            for s in range(pairs):
-                wanted = anc_ref[0, goal * pairs + s]
-                origin = lax.div(lax.div(wanted, pairs), inner)
-                block = gathered[part][origin, lax.rem(wanted, pairs)]
-                if d == 0:
-                    taken[part][place, s] = block
-                else:
-                    offered[part][d, s] = block
-            if d > 0:
-                x_copy(part, d).start()
-        if part > 0:
-            finish(part - 1)
+            if t == 1 and part + 3 < parts:
+                start_own(part + 3, middle)
+        part = turn - (outer - 2)
+        if part >= 0:
+            deliver(part)
+            if part > 0:
+                finish(part - 1)
     finish(parts - 1)
 
     for d in range(1, n):
@@ -369,13 +435,18 @@
     for part in range(parts):
         for d in range(1, inner):
             x_copy(part, d).wait_send()
+
+        @pl.when((line == 1) | (line == outer - 2))
+        def _(part=part):
+            end_copy(part).wait_send()
+
         for t in range(outer):
 
-            @pl.when((line - t >= 0) & (line < outer - 1))
+            @pl.when((line - t >= 0) & (line < outer - 2))
             def _(part=part, t=t):
                 z_copy(part, line - t, True).wait_send()
 
-            @pl.when((line + t < outer) & (line > 0))
+            @pl.when((line + t < outer) & (line > 1))
             def _(part=part, t=t):
                 z_copy(part, line + t, False).wait_send()
 
@@ -408,6 +479,7 @@
     ]
     scratch += [pltpu.VMEM((outer, pairs) + plane, f32)] * parts
     scratch += [pltpu.VMEM((inner, pairs) + plane, f32)] * (2 * parts)
+    scratch += [pltpu.VMEM((inner * pairs,) + plane, f32)] * (2 * parts)
     scratch += [
         dma((7,)),
         dma((7,)),
@@ -417,6 +489,8 @@
         dma((2, parts, outer)),
         dma((parts, inner)),
         dma((parts, inner)),
+        dma((parts,)),
+        dma((parts,)),
     ]
     resampled, weights = pl.pallas_call(
         functools.partial(kernel, (n, inner, outer, members, count_x, count_y)),

time: 83.8 us -> 77.6 us (0.926)
  Pallas kernels: 78.8 us -> 72.7 us
    pallas_call x1, Pallas kernels: 78.8 us -> 72.7 us  [shards(): pl.pallas_call(functools.partial(kernel, (n, inner, outer, members, count...]
where the time goes in v2:
time: 77.6 us; the launch traced here: 77.4 us
  Pallas kernels  72.7 us (94%)
  local copies, waits for them, and re-layouts  4.1 us (5%)
    pallas_call x1, Pallas kernels, shards(): pl.pallas_call(functools.partial(kernel, (n, inner, outer, members, count...  72.7 us
    unnamed x12, local copies, waits for them, and re-layouts  4.1 us

profile of v2, /device:TPU:0, one launch (start us, length us, event | category | flops | bytes accessed | tf_op | source)
XLA Modules:
  0.0 77.4 jit_solution(13792595055901107178)
XLA Ops:
  0.6 0.0 copy-start.3
  0.6 0.0 copy-start.2
  0.7 0.0 copy-start.4
  0.7 0.7 copy-done.3
  1.3 0.0 copy-done.2
  1.3 0.0 copy-done.4
  1.3 0.0 copy-start
  1.3 1.1 %copy-done = f32[4,3,128,128]{3,2,1,0:T(8,128)S(1)} copy-done((f32[4,3,128,128]{3,2,1,0:T(8,128)S(1)}, f32[4,3,128,128]{3,2,1,0:T(8,128)}, u32[]{:S(2)}) %copy-start) | copy-done | bytes 786456
  2.5 0.0 copy-start.1
  2.5 0.9 %copy-done.1 = f32[2,128,128]{2,1,0:T(8,128)S(1)} copy-done((f32[2,128,128]{2,1,0:T(8,128)S(1)}, f32[2,128,128]{2,1,0:T(8,128)}, u32[]{:S(2)}) %copy-start.1) | copy-done | bytes 131096
  3.4 72.7 %shard_map.68 = (f32[4,3,128,128]{3,2,1,0:T(8,128)S(1)}, f32[1,4]{1,0:T(1,128)S(1)}) custom-call(f32[4,3,128,128]{3,2,1,0:T(8,128)S(1)} %copy-done, f32[2,128,128]{2,1,0:T(8,128)S(1)} %copy-done.1, s32[1,16]{1,0:T(1,128)S(1)} %bitcast.6, s32[1,256]{1,0:T(1,128)S(1)} %bitcast.4, f32[1,256]{1,0:T(1,128)S(1)} %bitcast.5), custom_call_target="tpu_custom_call" | custom-call | tf_op jit(solution)/shard_map/pallas_call | solution.py:495
  76.1 0.9 %copy.9 = f32[4,3,128,128]{3,2,1,0:T(8,128)} copy(f32[4,3,128,128]{3,2,1,0:T(8,128)S(1)} %get-tuple-element.8) | data formatting | bytes 1572864
  76.9 0.5 copy.10
Async XLA Ops:
  0.6 0.7 copy-start.3
  0.6 0.7 copy-start.2
  0.7 0.7 copy-start.4
  1.3 1.1 %copy-start = (f32[4,3,128,128]{3,2,1,0:T(8,128)S(1)}, f32[4,3,128,128]{3,2,1,0:T(8,128)}, u32[]{:S(2)}) copy-start(f32[4,3,128,128]{3,2,1,0:T(8,128)} %fields_ref.1) | copy-start | bytes 2359300
  2.5 0.9 %copy-start.1 = (f32[2,128,128]{2,1,0:T(8,128)S(1)}, f32[2,128,128]{2,1,0:T(8,128)}, u32[]{:S(2)}) copy-start(f32[2,128,128]{2,1,0:T(8,128)} %noise_ref.1) | copy-start | bytes 393220

commit v3 on v2

--- a/solution.py
+++ b/solution.py
@@ -14,6 +14,7 @@
 EDGE = 8
 STRIPE = 32
 CHUNK = 16
+LEAD = 9
 
 
 def roll_y(a, shift):
@@ -77,7 +78,8 @@
 ):
     n, inner, outer, members, count_x, count_y = cfg
     pairs = members // 2
-    parts = 6
+    parts = 12
+    strip = count_x // 2
     gathered = rest[0:parts]
     offered = rest[parts : 2 * parts]
     taken = rest[2 * parts : 3 * parts]
@@ -158,9 +160,6 @@
         )
     for copy in rims:
         copy.start()
-    for copy in rims[1:5]:
-        copy.wait_recv()
-
     total_y = 2 * count_y
 
     def turning(local):
@@ -172,9 +171,10 @@
 
     wide = (count_x + 2 * EDGE) // CHUNK
 
-    def first_step(e):
+    def first_step(e, low, stride, count):
         def body(i, carry):
-            p, at = lax.div(i, wide), pl.multiple_of(lax.rem(i, wide) * CHUNK + EDGE, EDGE)
+            p, k = lax.div(i, count), lax.rem(i, count) * stride + low
+            at = pl.multiple_of(k * CHUNK + EDGE, EDGE)
             m = 2 * p + e
             new = advance(
                 lambda comp, d: old[m, comp, pl.ds(at + d, CHUNK), :],
@@ -185,9 +185,12 @@
                 mid[m, comp, pl.ds(at, CHUNK), :] = new[comp]
             return carry
 
-        lax.fori_loop(0, pairs * wide, body, 0, unroll=3)
-
-    first_step(0)
+        lax.fori_loop(0, pairs * count, body, 0, unroll=2)
+
+    first_step(0, 1, 1, wide - 2)
+    for copy in rims[1:5]:
+        copy.wait_recv()
+    first_step(0, 0, wide - 1, 2)
 
     for start in (BASE - EDGE, top):
         rows = pl.ds(start, EDGE)
@@ -254,13 +257,14 @@
 
     for e in range(2):
         if e == 1:
-            first_step(1)
-        for p in range(pairs):
-            m = 2 * p + e
-
-            def second_step(i, carry, m=m, p=p, e=e):
-                row = pl.multiple_of(i * CHUNK, CHUNK)
-                at = row + BASE
+            first_step(1, 0, 1, wide)
+        for half in range(2):
+
+            def second_step(i, carry, e=e, half=half):
+                p = lax.div(i, strip // CHUNK)
+                m = 2 * p + e
+                row = pl.multiple_of(lax.rem(i, strip // CHUNK) * CHUNK, CHUNK)
+                at = row + (BASE + half * strip)
                 new = advance(
                     lambda comp, d: mid[m, comp, pl.ds(at + d, CHUNK), :],
                     force[p, pl.ds(at, CHUNK), :],
@@ -268,50 +272,19 @@
                 )
                 for comp in range(3):
                     seam = seam_new[comp, pl.ds(at, CHUNK), :]
-                    low, high = roll_y(seam, -(STRIPE * m + 8)), roll_y(seam, -(STRIPE * m + 24))
+                    low, high = jnp.zeros_like(seam), jnp.zeros_like(seam)
+                    for q in range(pairs):
+                        base = STRIPE * (2 * q + e)
+                        low = jnp.where(p == q, roll_y(seam, -(base + 8)), low)
+                        high = jnp.where(p == q, roll_y(seam, -(base + 24)), high)
                     whole = jnp.where(lane < 4, low, jnp.where(lane >= count_y - 4, high, new[comp]))
-                    gathered[3 * e + comp][line, p, pl.ds(row, CHUNK), :] = whole
+                    gathered[6 * e + 3 * half + comp][line, p, pl.ds(row, CHUNK), :] = whole
                 return carry
 
-            lax.fori_loop(0, count_x // CHUNK, second_step, 0, unroll=2)
-        for comp in range(3):
-            start_own(3 * e + comp, None if e == 0 else at_end)
-
-    cells = cells_ref[...]
-    hot_y = jnp.where(
-        lax.broadcasted_iota(jnp.int32, (count_y, cells.shape[1]), 0) == lax.rem(cells, count_y),
-        1.0,
-        0.0,
-    )
-    hot_x = lax.broadcasted_iota(jnp.int32, (count_x, cells.shape[1]), 0) == lax.div(cells, count_y)
-    tile_lane = lax.broadcasted_iota(jnp.int32, (8, 128), 1)
-    own = jnp.zeros((8, 128), jnp.float32)
-    for m in range(members):
-        picked = jnp.dot(
-            gathered[3 * (m % 2)][line, m // 2],
-            hot_y,
-            precision=lax.Precision.HIGHEST,
-            preferred_element_type=jnp.float32,
-        )
-        seen = jnp.sum(jnp.where(hot_x, picked, 0.0), axis=0, keepdims=True)
-        misfit = seen - values_ref[...]
-        logw = -2.0 * jnp.sum(misfit * misfit, axis=1, keepdims=True)
-        own = jnp.where(tile_lane == m, logw, own)
-    logw_out[...] = own
-    logw_all[mem] = own
-
-    def w_copy(d):
-        return pltpu.make_async_remote_copy(
-            src_ref=logw_out,
-            dst_ref=logw_all.at[mem],
-            send_sem=w_send.at[d],
-            recv_sem=w_recv.at[d],
-            device_id=(lax.rem(mem + d, n), gx, gy),
-            device_id_type=MESH,
-        )
-
-    for d in range(1, n):
-        w_copy(d).start()
+            lax.fori_loop(0, pairs * (strip // CHUNK), second_step, 0, unroll=2)
+            for comp in range(3):
+                part = 6 * e + 3 * half + comp
+                start_own(part, None if part < LEAD else at_end)
 
     def x_copy(part, d):
         return pltpu.make_async_remote_copy(
@@ -324,12 +297,12 @@
         )
 
     def finish(part):
-        e, comp = part // 3, part % 3
+        e, rows, comp = part // 6, pl.ds(part // 3 % 2 * strip, strip), part % 3
         for d in range(1, inner):
             x_copy(part, d).wait_recv()
         for s in range(pairs):
             source = lax.rem(lax.div(anc_ref[0, mem * pairs + s], pairs), inner)
-            out_ref[2 * s + e, comp] = taken[part][source, s]
+            out_ref[2 * s + e, comp, rows, :] = taken[part][source, s]
 
     def end_copy(part):
         end = jnp.where(line == 1, 0, outer - 1)
@@ -384,6 +357,45 @@
         for d in range(1, inner):
             x_copy(part, d).start()
 
+    def w_copy(d):
+        return pltpu.make_async_remote_copy(
+            src_ref=logw_out,
+            dst_ref=logw_all.at[mem],
+            send_sem=w_send.at[d],
+            recv_sem=w_recv.at[d],
+            device_id=(lax.rem(mem + d, n), gx, gy),
+            device_id_type=MESH,
+        )
+
+    def weigh():
+        cells = cells_ref[...]
+        hot_y = jnp.where(
+            lax.broadcasted_iota(jnp.int32, (count_y, cells.shape[1]), 0) == lax.rem(cells, count_y),
+            1.0,
+            0.0,
+        )
+        hot_x = lax.broadcasted_iota(jnp.int32, (count_x, cells.shape[1]), 0) == lax.div(cells, count_y)
+        tile_lane = lax.broadcasted_iota(jnp.int32, (8, 128), 1)
+        own = jnp.zeros((8, 128), jnp.float32)
+        for m in range(members):
+            seen = jnp.zeros(cells.shape, jnp.float32)
+            for half in range(2):
+                picked = jnp.dot(
+                    gathered[6 * (m % 2) + 3 * half][line, m // 2],
+                    hot_y,
+                    precision=lax.Precision.HIGHEST,
+                    preferred_element_type=jnp.float32,
+                )
+                here = hot_x[half * strip : (half + 1) * strip]
+                seen += jnp.sum(jnp.where(here, picked, 0.0), axis=0, keepdims=True)
+            misfit = seen - values_ref[...]
+            logw = -2.0 * jnp.sum(misfit * misfit, axis=1, keepdims=True)
+            own = jnp.where(tile_lane == m, logw, own)
+        logw_out[...] = own
+        logw_all[mem] = own
+        for d in range(1, n):
+            w_copy(d).start()
+
     middle = jnp.logical_not(at_end)
     for turn in range(parts + outer - 2):
         for t in range(1, outer):
@@ -407,8 +419,10 @@
                 def _():
                     z_copy(part, line + t, False).start()
 
-            if t == 1 and part + 3 < parts:
-                start_own(part + 3, middle)
+            if t == 1 and part + LEAD < parts:
+                start_own(part + LEAD, middle)
+        if turn == 2:
+            weigh()
         part = turn - (outer - 2)
         if part >= 0:
             deliver(part)
@@ -425,7 +439,7 @@
     peak = jnp.max(every_max, axis=1, keepdims=True)
     expo = jnp.where(real & once, jnp.exp(jnp.where(real, every - peak[None], 0.0)), 0.0)
     total = jnp.sum(jnp.sum(jnp.sum(expo, axis=0), axis=1, keepdims=True), axis=0, keepdims=True)
-    normal = own - peak - jnp.log(total)
+    normal = logw_out[...] - peak - jnp.log(total)
     weights_ref[...] = normal[0:1, 0:members]
 
     for copy in rims:
@@ -462,8 +476,8 @@
     f32 = jnp.float32
     vmem = pl.BlockSpec(memory_space=pltpu.VMEM)
     dma = pltpu.SemaphoreType.DMA
-    parts = 2 * comps
-    plane = (count_x, count_y)
+    parts = 4 * comps
+    plane = (count_x // 2, count_y)
     scratch = [
         pltpu.VMEM((members, 3, rows, count_y), f32),
         pltpu.VMEM((members, 3, rows, count_y), f32),
@@ -472,7 +486,7 @@
         pltpu.VMEM((4, rows, count_y), f32),
         pltpu.VMEM((3, rows, count_y), f32),
         pltpu.VMEM((3, rows, count_y), f32),
-        pltpu.VMEM(plane, f32),
+        pltpu.VMEM((count_x, count_y), f32),
         pltpu.VMEM((rows, count_y), f32),
         pltpu.VMEM((8, 128), f32),
         pltpu.VMEM((n, 8, 128), f32),

time: 77.6 us -> 78 us (level)
  no operation moved by 1% of the time
where the time goes in v3:
time: 78 us; the launch traced here: 77.8 us
  Pallas kernels  73.1 us (94%)
  local copies, waits for them, and re-layouts  4.1 us (5%)
    pallas_call x1, Pallas kernels, shards(): pl.pallas_call(functools.partial(kernel, (n, inner, outer, members, count...  73.1 us
    unnamed x12, local copies, waits for them, and re-layouts  4.1 us

profile of v3, /device:TPU:0, one launch (start us, length us, event | category | flops | bytes accessed | tf_op | source)
XLA Modules:
  0.0 77.8 jit_solution(24095667768533438)
XLA Ops:
  0.6 0.0 copy-start.3
  0.6 0.0 copy-start.2
  0.7 0.0 copy-start.4
  0.7 0.7 copy-done.3
  1.3 0.0 copy-done.2
  1.3 0.0 copy-done.4
  1.3 0.0 copy-start
  1.3 1.1 %copy-done = f32[4,3,128,128]{3,2,1,0:T(8,128)S(1)} copy-done((f32[4,3,128,128]{3,2,1,0:T(8,128)S(1)}, f32[4,3,128,128]{3,2,1,0:T(8,128)}, u32[]{:S(2)}) %copy-start) | copy-done | bytes 786456
  2.5 0.0 copy-start.1
  2.5 0.9 %copy-done.1 = f32[2,128,128]{2,1,0:T(8,128)S(1)} copy-done((f32[2,128,128]{2,1,0:T(8,128)S(1)}, f32[2,128,128]{2,1,0:T(8,128)}, u32[]{:S(2)}) %copy-start.1) | copy-done | bytes 131096
  3.4 73.1 %shard_map.68 = (f32[4,3,128,128]{3,2,1,0:T(8,128)S(1)}, f32[1,4]{1,0:T(1,128)S(1)}) custom-call(f32[4,3,128,128]{3,2,1,0:T(8,128)S(1)} %copy-done, f32[2,128,128]{2,1,0:T(8,128)S(1)} %copy-done.1, s32[1,16]{1,0:T(1,128)S(1)} %bitcast.6, s32[1,256]{1,0:T(1,128)S(1)} %bitcast.4, f32[1,256]{1,0:T(1,128)S(1)} %bitcast.5), custom_call_target="tpu_custom_call" | custom-call | tf_op jit(solution)/shard_map/pallas_call | solution.py:509
  76.4 0.9 %copy.9 = f32[4,3,128,128]{3,2,1,0:T(8,128)} copy(f32[4,3,128,128]{3,2,1,0:T(8,128)S(1)} %get-tuple-element.8) | data formatting | bytes 1572864
  77.3 0.5 copy.10
Async XLA Ops:
  0.6 0.7 copy-start.3
  0.6 0.7 copy-start.2
  0.7 0.7 copy-start.4
  1.3 1.1 %copy-start = (f32[4,3,128,128]{3,2,1,0:T(8,128)S(1)}, f32[4,3,128,128]{3,2,1,0:T(8,128)}, u32[]{:S(2)}) copy-start(f32[4,3,128,128]{3,2,1,0:T(8,128)} %fields_ref.1) | copy-start | bytes 2359300
  2.5 0.9 %copy-start.1 = (f32[2,128,128]{2,1,0:T(8,128)S(1)}, f32[2,128,128]{2,1,0:T(8,128)}, u32[]{:S(2)}) copy-start(f32[2,128,128]{2,1,0:T(8,128)} %noise_ref.1) | copy-start | bytes 393220

commit v4 on v2

--- a/solution.py
+++ b/solution.py
@@ -14,6 +14,7 @@
 EDGE = 8
 STRIPE = 32
 CHUNK = 16
+LEAD = 5
 
 
 def roll_y(a, shift):
@@ -275,7 +276,7 @@
 
             lax.fori_loop(0, count_x // CHUNK, second_step, 0, unroll=2)
         for comp in range(3):
-            start_own(3 * e + comp, None if e == 0 else at_end)
+            start_own(3 * e + comp, None if 3 * e + comp < LEAD else at_end)
 
     cells = cells_ref[...]
     hot_y = jnp.where(
@@ -407,7 +408,7 @@
                 def _():
                     z_copy(part, line + t, False).start()
 
-            if t == 1 and part + 3 < parts:
+            if t == 1 and LEAD <= part + 3 < parts:
                 start_own(part + 3, middle)
         part = turn - (outer - 2)
         if part >= 0:

time: 77.6 us -> 80.4 us (1.036)
  Pallas kernels: 72.7 us -> 75.5 us
    pallas_call x1, Pallas kernels: 72.7 us -> 75.5 us  [shards(): pl.pallas_call(functools.partial(kernel, (n, inner, outer, members, count...]
where the time goes in v4:
time: 80.4 us; the launch traced here: 80.3 us
  Pallas kernels  75.5 us (94%)
  local copies, waits for them, and re-layouts  4.1 us (5%)
    pallas_call x1, Pallas kernels, shards(): pl.pallas_call(functools.partial(kernel, (n, inner, outer, members, count...  75.5 us
    unnamed x12, local copies, waits for them, and re-layouts  4.1 us

profile of v4, /device:TPU:0, one launch (start us, length us, event | category | flops | bytes accessed | tf_op | source)
XLA Modules:
  0.0 80.3 jit_solution(5826119455282472032)
XLA Ops:
  0.6 0.0 copy-start.3
  0.6 0.0 copy-start.2
  0.7 0.0 copy-start.4
  0.7 0.7 copy-done.3
  1.3 0.0 copy-done.2
  1.3 0.0 copy-done.4
  1.3 0.0 copy-start
  1.3 1.1 %copy-done = f32[4,3,128,128]{3,2,1,0:T(8,128)S(1)} copy-done((f32[4,3,128,128]{3,2,1,0:T(8,128)S(1)}, f32[4,3,128,128]{3,2,1,0:T(8,128)}, u32[]{:S(2)}) %copy-start) | copy-done | bytes 786456
  2.5 0.0 copy-start.1
  2.5 0.9 %copy-done.1 = f32[2,128,128]{2,1,0:T(8,128)S(1)} copy-done((f32[2,128,128]{2,1,0:T(8,128)S(1)}, f32[2,128,128]{2,1,0:T(8,128)}, u32[]{:S(2)}) %copy-start.1) | copy-done | bytes 131096
  3.4 75.5 %shard_map.68 = (f32[4,3,128,128]{3,2,1,0:T(8,128)S(1)}, f32[1,4]{1,0:T(1,128)S(1)}) custom-call(f32[4,3,128,128]{3,2,1,0:T(8,128)S(1)} %copy-done, f32[2,128,128]{2,1,0:T(8,128)S(1)} %copy-done.1, s32[1,16]{1,0:T(1,128)S(1)} %bitcast.6, s32[1,256]{1,0:T(1,128)S(1)} %bitcast.4, f32[1,256]{1,0:T(1,128)S(1)} %bitcast.5), custom_call_target="tpu_custom_call" | custom-call | tf_op jit(solution)/shard_map/pallas_call | solution.py:496
  78.9 0.9 %copy.9 = f32[4,3,128,128]{3,2,1,0:T(8,128)} copy(f32[4,3,128,128]{3,2,1,0:T(8,128)S(1)} %get-tuple-element.8) | data formatting | bytes 1572864
  79.7 0.5 copy.10
Async XLA Ops:
  0.6 0.7 copy-start.3
  0.6 0.7 copy-start.2
  0.7 0.7 copy-start.4
  1.3 1.1 %copy-start = (f32[4,3,128,128]{3,2,1,0:T(8,128)S(1)}, f32[4,3,128,128]{3,2,1,0:T(8,128)}, u32[]{:S(2)}) copy-start(f32[4,3,128,128]{3,2,1,0:T(8,128)} %fields_ref.1) | copy-start | bytes 2359300
  2.5 0.9 %copy-start.1 = (f32[2,128,128]{2,1,0:T(8,128)S(1)}, f32[2,128,128]{2,1,0:T(8,128)}, u32[]{:S(2)}) copy-start(f32[2,128,128]{2,1,0:T(8,128)} %noise_ref.1) | copy-start | bytes 393220

commit v5 on v3

--- a/solution.py
+++ b/solution.py
@@ -14,7 +14,8 @@
 EDGE = 8
 STRIPE = 32
 CHUNK = 16
-LEAD = 9
+LEAD = 3
+EARLY = {(0, 1): 0, (1, 0): 2, (1, 1): 3}
 
 
 def roll_y(a, shift):
@@ -255,37 +256,6 @@
         def _():
             z_copy(part, line, False).start()
 
-    for e in range(2):
-        if e == 1:
-            first_step(1, 0, 1, wide)
-        for half in range(2):
-
-            def second_step(i, carry, e=e, half=half):
-                p = lax.div(i, strip // CHUNK)
-                m = 2 * p + e
-                row = pl.multiple_of(lax.rem(i, strip // CHUNK) * CHUNK, CHUNK)
-                at = row + (BASE + half * strip)
-                new = advance(
-                    lambda comp, d: mid[m, comp, pl.ds(at + d, CHUNK), :],
-                    force[p, pl.ds(at, CHUNK), :],
-                    cor_tile,
-                )
-                for comp in range(3):
-                    seam = seam_new[comp, pl.ds(at, CHUNK), :]
-                    low, high = jnp.zeros_like(seam), jnp.zeros_like(seam)
-                    for q in range(pairs):
-                        base = STRIPE * (2 * q + e)
-                        low = jnp.where(p == q, roll_y(seam, -(base + 8)), low)
-                        high = jnp.where(p == q, roll_y(seam, -(base + 24)), high)
-                    whole = jnp.where(lane < 4, low, jnp.where(lane >= count_y - 4, high, new[comp]))
-                    gathered[6 * e + 3 * half + comp][line, p, pl.ds(row, CHUNK), :] = whole
-                return carry
-
-            lax.fori_loop(0, pairs * (strip // CHUNK), second_step, 0, unroll=2)
-            for comp in range(3):
-                part = 6 * e + 3 * half + comp
-                start_own(part, None if part < LEAD else at_end)
-
     def x_copy(part, d):
         return pltpu.make_async_remote_copy(
             src_ref=offered[part].at[d],
@@ -397,7 +367,7 @@
             w_copy(d).start()
 
     middle = jnp.logical_not(at_end)
-    for turn in range(parts + outer - 2):
+    def take_turn(turn):
         for t in range(1, outer):
             part = turn - (t - 1)
             if not 0 <= part < parts:
@@ -421,13 +391,50 @@
 
             if t == 1 and part + LEAD < parts:
                 start_own(part + LEAD, middle)
-        if turn == 2:
+        if turn == 4:
             weigh()
         part = turn - (outer - 2)
         if part >= 0:
             deliver(part)
             if part > 0:
                 finish(part - 1)
+
+    for e in range(2):
+        if e == 1:
+            first_step(1, 0, 1, wide)
+            take_turn(1)
+        for half in range(2):
+
+            def second_step(i, carry, e=e, half=half):
+                p = lax.div(i, strip // CHUNK)
+                m = 2 * p + e
+                row = pl.multiple_of(lax.rem(i, strip // CHUNK) * CHUNK, CHUNK)
+                at = row + (BASE + half * strip)
+                new = advance(
+                    lambda comp, d: mid[m, comp, pl.ds(at + d, CHUNK), :],
+                    force[p, pl.ds(at, CHUNK), :],
+                    cor_tile,
+                )
+                for comp in range(3):
+                    seam = seam_new[comp, pl.ds(at, CHUNK), :]
+                    low, high = jnp.zeros_like(seam), jnp.zeros_like(seam)
+                    for q in range(pairs):
+                        base = STRIPE * (2 * q + e)
+                        low = jnp.where(p == q, roll_y(seam, -(base + 8)), low)
+                        high = jnp.where(p == q, roll_y(seam, -(base + 24)), high)
+                    whole = jnp.where(lane < 4, low, jnp.where(lane >= count_y - 4, high, new[comp]))
+                    gathered[6 * e + 3 * half + comp][line, p, pl.ds(row, CHUNK), :] = whole
+                return carry
+
+            lax.fori_loop(0, pairs * (strip // CHUNK), second_step, 0, unroll=2)
+            for comp in range(3):
+                part = 6 * e + 3 * half + comp
+                start_own(part, None if part < LEAD else at_end)
+            if (e, half) in EARLY:
+                take_turn(EARLY[e, half])
+
+    for turn in range(4, parts + outer - 2):
+        take_turn(turn)
     finish(parts - 1)
 
     for d in range(1, n):

time: 78 us -> 69.8 us (0.89)
  Pallas kernels: 73.1 us -> 64.9 us
    pallas_call x1, Pallas kernels: 73.1 us -> 64.9 us  [shards(): pl.pallas_call(functools.partial(kernel, (n, inner, outer, members, count...]
where the time goes in v5:
time: 69.8 us; the launch traced here: 69.6 us
  Pallas kernels  64.9 us (93%)
  local copies, waits for them, and re-layouts  4.1 us (6%)
    pallas_call x1, Pallas kernels, shards(): pl.pallas_call(functools.partial(kernel, (n, inner, outer, members, count...  64.9 us
    unnamed x12, local copies, waits for them, and re-layouts  4.1 us

profile of v5, /device:TPU:0, one launch (start us, length us, event | category | flops | bytes accessed | tf_op | source)
XLA Modules:
  0.0 69.6 jit_solution(16775960215683902521)
XLA Ops:
  0.6 0.0 copy-start.3
  0.6 0.0 copy-start.2
  0.7 0.0 copy-start.4
  0.7 0.7 copy-done.3
  1.3 0.0 copy-done.2
  1.3 0.0 copy-done.4
  1.3 0.0 copy-start
  1.3 1.1 %copy-done = f32[4,3,128,128]{3,2,1,0:T(8,128)S(1)} copy-done((f32[4,3,128,128]{3,2,1,0:T(8,128)S(1)}, f32[4,3,128,128]{3,2,1,0:T(8,128)}, u32[]{:S(2)}) %copy-start) | copy-done | bytes 786456
  2.5 0.0 copy-start.1
  2.5 0.9 %copy-done.1 = f32[2,128,128]{2,1,0:T(8,128)S(1)} copy-done((f32[2,128,128]{2,1,0:T(8,128)S(1)}, f32[2,128,128]{2,1,0:T(8,128)}, u32[]{:S(2)}) %copy-start.1) | copy-done | bytes 131096
  3.4 64.9 %shard_map.68 = (f32[4,3,128,128]{3,2,1,0:T(8,128)S(1)}, f32[1,4]{1,0:T(1,128)S(1)}) custom-call(f32[4,3,128,128]{3,2,1,0:T(8,128)S(1)} %copy-done, f32[2,128,128]{2,1,0:T(8,128)S(1)} %copy-done.1, s32[1,16]{1,0:T(1,128)S(1)} %bitcast.6, s32[1,256]{1,0:T(1,128)S(1)} %bitcast.4, f32[1,256]{1,0:T(1,128)S(1)} %bitcast.5), custom_call_target="tpu_custom_call" | custom-call | tf_op jit(solution)/shard_map/pallas_call | solution.py:516
  68.3 0.9 %copy.9 = f32[4,3,128,128]{3,2,1,0:T(8,128)} copy(f32[4,3,128,128]{3,2,1,0:T(8,128)S(1)} %get-tuple-element.8) | data formatting | bytes 1572864
  69.1 0.5 copy.10
Async XLA Ops:
  0.6 0.7 copy-start.3
  0.6 0.7 copy-start.2
  0.7 0.7 copy-start.4
  1.3 1.1 %copy-start = (f32[4,3,128,128]{3,2,1,0:T(8,128)S(1)}, f32[4,3,128,128]{3,2,1,0:T(8,128)}, u32[]{:S(2)}) copy-start(f32[4,3,128,128]{3,2,1,0:T(8,128)} %fields_ref.1) | copy-start | bytes 2359300
  2.5 0.9 %copy-start.1 = (f32[2,128,128]{2,1,0:T(8,128)S(1)}, f32[2,128,128]{2,1,0:T(8,128)}, u32[]{:S(2)}) copy-start(f32[2,128,128]{2,1,0:T(8,128)} %noise_ref.1) | copy-start | bytes 393220

commit v6 on v5

--- a/solution.py
+++ b/solution.py
@@ -367,6 +367,7 @@
             w_copy(d).start()
 
     middle = jnp.logical_not(at_end)
+
     def take_turn(turn):
         for t in range(1, outer):
             part = turn - (t - 1)
@@ -392,7 +393,7 @@
             if t == 1 and part + LEAD < parts:
                 start_own(part + LEAD, middle)
         if turn == 4:
-            weigh()
+            pl.when(at_end)(weigh)
         part = turn - (outer - 2)
         if part >= 0:
             deliver(part)
@@ -405,10 +406,9 @@
             take_turn(1)
         for half in range(2):
 
-            def second_step(i, carry, e=e, half=half):
-                p = lax.div(i, strip // CHUNK)
+            def second_step(i, carry, p, e=e, half=half):
                 m = 2 * p + e
-                row = pl.multiple_of(lax.rem(i, strip // CHUNK) * CHUNK, CHUNK)
+                row = pl.multiple_of(i * CHUNK, CHUNK)
                 at = row + (BASE + half * strip)
                 new = advance(
                     lambda comp, d: mid[m, comp, pl.ds(at + d, CHUNK), :],
@@ -417,16 +417,14 @@
                 )
                 for comp in range(3):
                     seam = seam_new[comp, pl.ds(at, CHUNK), :]
-                    low, high = jnp.zeros_like(seam), jnp.zeros_like(seam)
-                    for q in range(pairs):
-                        base = STRIPE * (2 * q + e)
-                        low = jnp.where(p == q, roll_y(seam, -(base + 8)), low)
-                        high = jnp.where(p == q, roll_y(seam, -(base + 24)), high)
+                    low, high = roll_y(seam, -(STRIPE * m + 8)), roll_y(seam, -(STRIPE * m + 24))
                     whole = jnp.where(lane < 4, low, jnp.where(lane >= count_y - 4, high, new[comp]))
                     gathered[6 * e + 3 * half + comp][line, p, pl.ds(row, CHUNK), :] = whole
                 return carry
 
-            lax.fori_loop(0, pairs * (strip // CHUNK), second_step, 0, unroll=2)
+            for p in range(pairs):
+                body = functools.partial(second_step, p=p)
+                lax.fori_loop(0, strip // CHUNK, body, 0, unroll=2)
             for comp in range(3):
                 part = 6 * e + 3 * half + comp
                 start_own(part, None if part < LEAD else at_end)
@@ -435,6 +433,7 @@
 
     for turn in range(4, parts + outer - 2):
         take_turn(turn)
+    pl.when(middle)(weigh)
     finish(parts - 1)
 
     for d in range(1, n):

time: 69.8 us -> 69.5 us (level)
  no operation moved by 1% of the time
where the time goes in v6:
time: 69.5 us; the launch traced here: 69.3 us
  Pallas kernels  64.5 us (93%)
  local copies, waits for them, and re-layouts  4.1 us (6%)
    pallas_call x1, Pallas kernels, shards(): pl.pallas_call(functools.partial(kernel, (n, inner, outer, members, count...  64.5 us
    unnamed x12, local copies, waits for them, and re-layouts  4.1 us

profile of v6, /device:TPU:0, one launch (start us, length us, event | category | flops | bytes accessed | tf_op | source)
XLA Modules:
  0.0 69.3 jit_solution(6271459630045729849)
XLA Ops:
  0.6 0.0 copy-start.3
  0.6 0.0 copy-start.2
  0.7 0.0 copy-start.4
  0.7 0.7 copy-done.3
  1.3 0.0 copy-done.2
  1.3 0.0 copy-done.4
  1.3 0.0 copy-start
  1.3 1.1 %copy-done = f32[4,3,128,128]{3,2,1,0:T(8,128)S(1)} copy-done((f32[4,3,128,128]{3,2,1,0:T(8,128)S(1)}, f32[4,3,128,128]{3,2,1,0:T(8,128)}, u32[]{:S(2)}) %copy-start) | copy-done | bytes 786456
  2.5 0.0 copy-start.1
  2.5 0.9 %copy-done.1 = f32[2,128,128]{2,1,0:T(8,128)S(1)} copy-done((f32[2,128,128]{2,1,0:T(8,128)S(1)}, f32[2,128,128]{2,1,0:T(8,128)}, u32[]{:S(2)}) %copy-start.1) | copy-done | bytes 131096
  3.4 64.5 %shard_map.68 = (f32[4,3,128,128]{3,2,1,0:T(8,128)S(1)}, f32[1,4]{1,0:T(1,128)S(1)}) custom-call(f32[4,3,128,128]{3,2,1,0:T(8,128)S(1)} %copy-done, f32[2,128,128]{2,1,0:T(8,128)S(1)} %copy-done.1, s32[1,16]{1,0:T(1,128)S(1)} %bitcast.6, s32[1,256]{1,0:T(1,128)S(1)} %bitcast.4, f32[1,256]{1,0:T(1,128)S(1)} %bitcast.5), custom_call_target="tpu_custom_call" | custom-call | tf_op jit(solution)/shard_map/pallas_call | solution.py:515
  67.9 0.9 %copy.9 = f32[4,3,128,128]{3,2,1,0:T(8,128)} copy(f32[4,3,128,128]{3,2,1,0:T(8,128)S(1)} %get-tuple-element.8) | data formatting | bytes 1572864
  68.8 0.5 copy.10
Async XLA Ops:
  0.6 0.7 copy-start.3
  0.6 0.7 copy-start.2
  0.7 0.7 copy-start.4
  1.3 1.1 %copy-start = (f32[4,3,128,128]{3,2,1,0:T(8,128)S(1)}, f32[4,3,128,128]{3,2,1,0:T(8,128)}, u32[]{:S(2)}) copy-start(f32[4,3,128,128]{3,2,1,0:T(8,128)} %fields_ref.1) | copy-start | bytes 2359300
  2.5 0.9 %copy-start.1 = (f32[2,128,128]{2,1,0:T(8,128)S(1)}, f32[2,128,128]{2,1,0:T(8,128)}, u32[]{:S(2)}) copy-start(f32[2,128,128]{2,1,0:T(8,128)} %noise_ref.1) | copy-start | bytes 393220
